TPU v7x, 128 devices: a whole 4x4x4 slice. The times are simulated.
128 devices in a mesh: leaf: 32 (over y_lo, x, z), pts: 4 (over y_hi, core).
Axes of the slice: x: 4, y: 4 (y_hi: 2, y_lo: 2; y = y_hi * 2 + y_lo), z: 4, core: 2. Of those that a mesh axis runs over, the one named last changes fastest.
Arguments:
- points_rhs: float32 [524288, 512], P(('leaf', 'pts')), may hold values from -6 to 6
- order: int32 [128, 4096], P(('leaf', 'pts')), may hold values from 0 to 4095, each once within a row
- basis: float32 [524288, 256], P(('leaf', 'pts')), may hold values from -0.046875 to 0.046875
- near_blocks: float32 [8192, 128, 128], P(('leaf', 'pts')), may hold values from -0.375 to 0.375
- near_pairs: int32 [8192, 2], P(('leaf', 'pts')), may hold values from 0 to 33, as said below
- transfer: float32 [32, 4, 256, 256], P('leaf'), may hold values from -0.375 to 0.375
- coupling: float32 [32, 5, 256, 256], P('leaf'), may hold values from -0.375 to 0.375
Outputs:
- product: float32 [524288, 512], P(('leaf', 'pts'))
Inputs may be any that keep to these rules, and one draw needn't show every extreme that they name: `near_pairs`: each device's 64 pairs (r, c) have r in 0 .. 31 and c in r .. r + 2; every row block appears; row block 0 appears with column block 0 and the last row block with the last column block. `order`: each device's row is a permutation of 0 .. 4095.
All inputs are finite; a program needn't handle non-finite values.
Results may differ from a plain program's by a relative error of at most 0.0003.
Values sent between devices are 32-bit elements; how exact they have to be, the bound alone decides.
A program may use at most 192 MiB of HBM per device.

v0:
```python
import functools

import jax
import jax.numpy as jnp
from jax import lax
from jax.experimental import pallas as pl
from jax.experimental.pallas import tpu as pltpu
from jax.sharding import PartitionSpec as P

MESH = pl.DeviceIdType.MESH
F32, BF16, I32 = jnp.float32, jnp.bfloat16, jnp.int32
LANES, SUB = 128, 8
MIB = 2**20
CHUNK = 256
HALVES = 2


def split(x):
    hi = x.astype(BF16)
    return hi, (x - hi.astype(F32)).astype(BF16)


def stack(x):
    return jnp.concatenate(split(x), axis=0)


def dot(a, b):
    return jnp.dot(a, b, preferred_element_type=F32)


def dot_t(a, b):
    return lax.dot_general(a, b, (((1,), (1,)), ((), ())), preferred_element_type=F32)


def three(mul, a, bh, bl):
    n = a.shape[0] // 2
    both = mul(a, bh)
    return both[:n] + (both[n:] + mul(a[:n], bl))


def row_address(order, tiles):
    return (order >> 3) * (SUB * tiles) + (order & (SUB - 1))


def tiles_of(ref, tiles, first, count):
    return [
        jnp.concatenate([ref[(g * tiles + j) * SUB:(g * tiles + j + 1) * SUB, :]
                         for g in range(first // SUB, (first + count) // SUB)], axis=0)
        for j in range(tiles)
    ]


def tree_kernel(levels, order_in, pairs_in, x_hbm, basis_hbm, blocks_hbm, t_hbm, g_hbm, d_out, near_hbm,
                xv, bv, bt, rows_a, rows_b, acc, cin, edge, ph, pl_, blk, pre, nv,
                tv, gv, tsib, wt, ws, wf, addr_v, addr, key_v, tab_v, tab,
                rs1, stage, rs2, cb, crecv, own, ebuf, dbuf, erecv,
                in_sem, n_sem, t_send, t_recv, r_send, r_recv, c_send, c_recv, d_send, d_recv, e_send, e_recv):
    rows, cols = nv.shape
    rank = bv.shape[1]
    tiles = cols // LANES
    count, size = blk.shape[0], blk.shape[1]
    row_blocks = rows // size
    width = cin.shape[1]
    half = width // HALVES
    chunks = rows // CHUNK
    leaf, p = lax.axis_index("leaf"), lax.axis_index("pts")
    parts = cin.shape[0]
    top = levels - 1
    core, far_chip = (leaf, p ^ 1), (leaf, p ^ 2)
    following, before = (leaf, lax.rem(p + 1, parts)), (leaf, lax.rem(p + parts - 1, parts))
    siblings = [(leaf ^ (1 << l), p) for l in range(levels)]

    def load(src, dst, i):
        copy = pltpu.make_async_copy(src, dst, in_sem.at[i])
        copy.start()
        return copy

    def send(src, dst, to, send_sem, recv_sem):
        copy = pltpu.make_async_remote_copy(
            src_ref=src, dst_ref=dst, send_sem=send_sem, recv_sem=recv_sem, device_id=to, device_id_type=MESH)
        copy.start()
        return copy

    barrier = pltpu.get_barrier_semaphore()
    greeted = [core, far_chip, (leaf, p ^ 3)] + siblings
    for other in greeted:
        pl.semaphore_signal(barrier, inc=1, device_id=other, device_id_type=MESH)
    in_t = load(t_hbm, tv, 0)
    in_g = load(g_hbm, gv, 1)
    in_b = load(basis_hbm, bv, 2)
    in_x = load(x_hbm, xv, 3)
    in_k = load(blocks_hbm, blk, 4)
    addr_v[...] = row_address(order_in[...], tiles)
    in_a = load(addr_v, addr, 5)

    key_v[...] = jnp.full(key_v.shape, 1e6, F32)
    key_v[0:1, :count] = (2 * pairs_in[0:1, :] + pairs_in[1:2, :]).astype(F32)
    across = jnp.broadcast_to(key_v[0:1, :], (LANES, LANES))
    down_key = across.T
    row_i = lax.broadcasted_iota(I32, (LANES, LANES), 0)
    col_i = lax.broadcasted_iota(I32, (LANES, LANES), 1)
    col_f = col_i.astype(F32)
    one = lambda cond: jnp.where(cond, 1.0, 0.0)
    twin = one((across == down_key) & (col_i < row_i))
    place = jnp.sum(twin + one(across < down_key), axis=1, keepdims=True)
    hit = one(place == col_f)
    again = jnp.where(jnp.sum(twin, axis=1, keepdims=True) > 0, 1.0, 0.0)
    total = lambda x: jnp.sum(x, axis=0, keepdims=True)
    found = total(one(down_key == col_f))
    last = jnp.where(found > 0, total(one(down_key <= col_f)) - 1.0, float(count))
    tab_v[...] = jnp.zeros_like(tab_v)
    tab_v[0:1, :] = total(hit * row_i.astype(F32)).astype(I32)
    tab_v[1:2, :] = total(hit * again).astype(I32)
    tab_v[2:3, :] = last.astype(I32)
    in_tab = load(tab_v, tab, 6)
    pre[0] = jnp.zeros((size, size), F32)
    pre[count] = jnp.zeros((size, size), F32)
    acc[...] = jnp.zeros_like(acc)

    pl.semaphore_wait(barrier, len(greeted))
    moved = [send(t_hbm.at[l], tsib.at[l], siblings[l], t_send.at[l], t_recv.at[l]) for l in range(top)]

    in_t.wait()
    in_g.wait()
    for l in range(top):
        wt[l, 0], wt[l, 1] = split(tv[l])
    wf[...] = tv[0]
    ws[0, 0], ws[0, 1] = split(gv[0])
    for l in range(1, levels):
        path = stack(wf[...])
        gh, gl = split(gv[l])
        ws[l, 0], ws[l, 1] = split(three(dot, path, gh, gl))
        if l < top:
            wf[...] = three(dot, path, wt[l, 0], wt[l, 1])

    in_b.wait()

    @pl.loop(0, chunks)
    def _(i):
        at = pl.multiple_of(i * CHUNK, CHUNK)
        bt[:, pl.ds(at, CHUNK)] = stack(bv[pl.ds(at, CHUNK), :].T)

    in_a.wait()
    in_tab.wait()
    in_x.wait()

    def gather(i, buf):
        step = 32
        for g in range(CHUNK // step):
            ids = [g * step + u for u in range(step)]
            vals = [xv[pl.ds(addr[i * (CHUNK // LANES) + k // LANES, k % LANES], tiles, stride=SUB), :] for k in ids]
            for k, val in zip(ids, vals):
                buf[pl.ds((k // SUB) * (SUB * tiles) + k % SUB, tiles, stride=SUB), :] = val

    def compress(i, buf):
        at = pl.multiple_of(i * CHUNK, CHUNK)
        hi, lo = zip(*[split(part) for part in tiles_of(buf, tiles, 0, CHUNK)])
        hi, lo = jnp.concatenate(hi, axis=1), jnp.concatenate(lo, axis=1)
        to = pl.ds(pl.multiple_of(size + at, size), CHUNK)
        ph[to, :] = hi
        pl_[to, :] = lo
        acc[...] += three(dot, bt[:, pl.ds(at, CHUNK)], hi, lo)

    gather(0, rows_a)
    for j, part in enumerate(tiles_of(rows_a, tiles, 0, size)):
        edge[0, :, j * LANES:(j + 1) * LANES] = part

    @pl.loop(0, chunks // 2 - 1)
    def _(i):
        gather(2 * i + 1, rows_b)
        compress(2 * i, rows_a)
        gather(2 * i + 2, rows_a)
        compress(2 * i + 1, rows_b)

    gather(chunks - 1, rows_b)
    compress(chunks - 2, rows_a)
    for j, part in enumerate(tiles_of(rows_b, tiles, CHUNK - size, size)):
        edge[1, :, j * LANES:(j + 1) * LANES] = part
    compress(chunks - 1, rows_b)
    for q in range(parts):
        cin[q] = acc[:, q * width:(q + 1) * width].T

    hs = [pl.ds(h * half, half) for h in range(HALVES)]
    to_core = [[send(cin.at[p ^ (3 - 2 * k), hs[h]], rs1.at[k, hs[h]], core, r_send.at[k, h], r_recv.at[k, h])
                for h in range(HALVES)] for k in range(2)]
    to_far = []
    for h in range(HALVES):
        to_core[0][h].wait_recv()
        stage[hs[h], :] = cin[p ^ 2, hs[h], :] + rs1[0, hs[h], :]
        to_far.append(send(stage.at[hs[h]], rs2.at[hs[h]], far_chip, r_send.at[2, h], r_recv.at[2, h]))
    for copy in to_core[1]:
        copy.wait_recv()
    sent = to_core[0] + to_core[1] + to_far + moved

    in_k.wait()

    @pl.loop(0, count)
    def _(m):
        pre[m] = jnp.where(tab[1, m] > 0, pre[jnp.maximum(m - 1, 0)], 0.0) + blk[jnp.clip(tab[0, m], 0, count - 1)]

    outs = []

    def near(first, number):
        if not number:
            return

        @pl.loop(first, first + number)
        def _(u):
            none = jnp.zeros((size, size), F32)
            get = lambda r, o: pre[jnp.clip(tab[2, 6 * u + 3 * r + o], 0, count)]
            upper = jnp.concatenate([get(0, 0), get(0, 1), get(0, 2), none], axis=1)
            lower = jnp.concatenate([none, get(1, 0), get(1, 1), get(1, 2)], axis=1)
            band = stack(jnp.concatenate([upper, lower], axis=0))
            at = pl.multiple_of(u * (2 * size), 2 * size)
            span = pl.ds(at, 4 * size)
            nv[pl.ds(at, 2 * size), :] = three(dot, band, ph[span, :], pl_[span, :])

        span = pl.ds(first * 2 * size, number * 2 * size)
        out = pltpu.make_async_copy(nv.at[span], near_hbm.at[span], n_sem.at[first])
        out.start()
        outs.append(out)

    units = row_blocks // 2
    inner = units - 2
    cuts = [1 + inner * i // (levels + 1) for i in range(levels + 2)]

    def near_step(i):
        near(cuts[i], cuts[i + 1] - cuts[i])

    near_step(0)
    for l in range(top):
        moved[l].wait_recv()
        wt[top + l, 0], wt[top + l, 1] = split(tsib[l])

    edges = []
    up = []
    for h in range(HALVES):
        to_far[h].wait_recv()
        cb[0, hs[h], :] = cin[p, hs[h], :] + (rs1[1, hs[h], :] + rs2[hs[h], :])
        up.append(send(cb.at[0, hs[h]], crecv.at[0, hs[h]], siblings[0], c_send.at[0, h], c_recv.at[0, h]))
    for l in range(top):
        if l == 0:
            edges.append(send(edge.at[1], erecv.at[0], following, e_send.at[0], e_recv.at[0]))
            edges.append(send(edge.at[0], erecv.at[1], before, e_send.at[1], e_recv.at[1]))
        own[...] = three(dot, stack(cb[l]), wt[l, 0], wt[l, 1])
        near_step(1 + l)
        for h in range(HALVES):
            up[l * HALVES + h].wait_recv()
            cb[l + 1, hs[h], :] = own[hs[h], :] + three(dot, stack(crecv[l, hs[h], :]), wt[top + l, 0], wt[top + l, 1])
            up.append(send(cb.at[l + 1, hs[h]], crecv.at[l + 1, hs[h]], siblings[l + 1], c_send.at[l + 1, h], c_recv.at[l + 1, h]))
        part = three(dot_t, stack(crecv[l]), ws[l, 0], ws[l, 1])
        ebuf[...] = part if l == 0 else ebuf[...] + part
    near_step(levels)
    d0, d1, d2 = [], [], []
    for h in range(HALVES):
        up[top * HALVES + h].wait_recv()
        dbuf[p, hs[h], :] = ebuf[hs[h], :] + three(dot_t, stack(crecv[top, hs[h], :]), ws[top, 0], ws[top, 1])
        mine = dbuf.at[p, hs[h]]
        d0.append(send(mine, mine, far_chip, d_send.at[0, h], d_recv.at[0, h]))
        d1.append(send(mine, mine, core, d_send.at[1, h], d_recv.at[1, h]))

    for copy in edges:
        copy.wait_recv()
    ph[:size, :], pl_[:size, :] = split(jnp.where(p == 0, 0.0, erecv[0]))
    ph[size + rows:, :], pl_[size + rows:, :] = split(jnp.where(p == parts - 1, 0.0, erecv[1]))
    near(0, 1)
    near(units - 1, 1)
    for h in range(HALVES):
        d0[h].wait_recv()
        other = dbuf.at[p ^ 2, hs[h]]
        d2.append(send(other, other, core, d_send.at[2, h], d_recv.at[2, h]))
    for copy in d1 + d2:
        copy.wait_recv()
    for q in range(parts):
        d_out[q * width:(q + 1) * width, :] = dbuf[q]
    for copy in sent + up + edges + d0 + d1 + d2:
        copy.wait_send()
    for out in outs:
        out.wait()


def tree_call(levels, parts, order, pairs, x, basis, blocks, transfer, coupling):
    rows, rank = basis.shape
    tiles = x.shape[0] // rows
    cols = tiles * LANES
    count, size = blocks.shape[0], blocks.shape[1]
    width = cols // parts
    hbm, vmem = (pl.BlockSpec(memory_space=s) for s in (pl.ANY, pltpu.VMEM))
    shape = jax.ShapeDtypeStruct
    dma = pltpu.SemaphoreType.DMA
    part = (width, rank)
    padded = (rows + 2 * size, cols)
    scratch = [
        (x.shape, F32), (basis.shape, F32), ((2 * rank, rows), BF16), ((CHUNK * tiles, LANES), F32), ((CHUNK * tiles, LANES), F32),
        ((rank, cols), F32), ((parts,) + part, F32), ((2, size, cols), F32), (padded, BF16), (padded, BF16),
        (blocks.shape, F32), ((count + 1, size, size), F32), ((rows, cols), F32),
        (transfer.shape, F32), (coupling.shape, F32), (transfer.shape, F32),
        ((2 * (levels - 1), 2, rank, rank), BF16), ((levels, 2, rank, rank), BF16), ((rank, rank), F32),
        (order.shape, I32), None, ((SUB, LANES), F32), ((SUB, LANES), I32), None,
        ((2,) + part, F32), (part, F32), (part, F32), ((levels,) + part, F32), ((levels,) + part, F32),
        (part, F32), (part, F32), ((parts,) + part, F32), ((2, size, cols), F32),
    ]
    scratch = [pltpu.VMEM(*s) if s else None for s in scratch]
    scratch[20] = pltpu.SMEM(order.shape, I32)
    scratch[23] = pltpu.SMEM((SUB, LANES), I32)
    return pl.pallas_call(
        functools.partial(tree_kernel, levels),
        out_shape=(shape((cols, rank), F32), shape((rows, cols), F32)),
        in_specs=[vmem, vmem, hbm, hbm, hbm, hbm, hbm],
        out_specs=(vmem, hbm),
        scratch_shapes=scratch + [
            dma((7,)), dma((rows // size,)), dma((levels - 1,)), dma((levels - 1,)), dma((3, HALVES)), dma((3, HALVES)),
            dma((levels, HALVES)), dma((levels, HALVES)), dma((3, HALVES)), dma((3, HALVES)), dma((2,)), dma((2,)),
        ],
        compiler_params=pltpu.CompilerParams(vmem_limit_bytes=60 * MIB, collective_id=0, has_side_effects=True),
        name="tree_near",
    )(order, pairs, x, basis, blocks, transfer, coupling)


def scatter_kernel(order_in, d_in, basis_hbm, near_hbm, out_hbm, bv, nv, ov, rows_a, rows_b, dh, dl, addr_v, addr, in_sem, a_sem, out_sem):
    rows, rank = bv.shape
    cols = nv.shape[1]
    tiles = cols // LANES
    chunks = rows // CHUNK

    def copies(i):
        at = pl.multiple_of(i * CHUNK, CHUNK)
        return (pltpu.make_async_copy(basis_hbm.at[pl.ds(at, CHUNK)], bv.at[pl.ds(at, CHUNK)], in_sem.at[0, i]),
                pltpu.make_async_copy(near_hbm.at[pl.ds(at, CHUNK)], nv.at[pl.ds(at, CHUNK)], in_sem.at[1, i]))

    @pl.loop(0, chunks)
    def _(i):
        for copy in copies(i):
            copy.start()

    addr_v[...] = row_address(order_in[...], tiles)
    in_a = pltpu.make_async_copy(addr_v, addr, a_sem)
    in_a.start()
    for j in range(tiles):
        h, l = split(d_in[j * LANES:(j + 1) * LANES, :].T)
        dh[:, j * LANES:(j + 1) * LANES] = h
        dl[:, j * LANES:(j + 1) * LANES] = l
    in_a.wait()

    def wait(i):
        for copy in copies(i):
            copy.wait()

    def multiply(i, buf):
        at = pl.multiple_of(i * CHUNK, CHUNK)
        total = nv[pl.ds(at, CHUNK), :] + three(dot, stack(bv[pl.ds(at, CHUNK), :]), dh[...], dl[...])
        for g in range(CHUNK // SUB):
            for j in range(tiles):
                buf[(g * tiles + j) * SUB:(g * tiles + j + 1) * SUB, :] = total[g * SUB:(g + 1) * SUB, j * LANES:(j + 1) * LANES]

    def scatter(i, buf):
        for k in range(CHUNK):
            to = addr[i * (CHUNK // LANES) + k // LANES, k % LANES]
            ov[pl.ds(to, tiles, stride=SUB), :] = buf[pl.ds((k // SUB) * (SUB * tiles) + k % SUB, tiles, stride=SUB), :]

    wait(0)
    multiply(0, rows_a)

    @pl.loop(0, chunks // 2 - 1)
    def _(i):
        wait(2 * i + 1)
        multiply(2 * i + 1, rows_b)
        scatter(2 * i, rows_a)
        wait(2 * i + 2)
        multiply(2 * i + 2, rows_a)
        scatter(2 * i + 1, rows_b)

    wait(chunks - 1)
    multiply(chunks - 1, rows_b)
    scatter(chunks - 2, rows_a)
    scatter(chunks - 1, rows_b)
    out = pltpu.make_async_copy(ov, out_hbm, out_sem)
    out.start()
    out.wait()


def scatter_call(order, down, basis, near):
    rows, rank = basis.shape
    cols = near.shape[1]
    tiles = cols // LANES
    hbm, vmem = (pl.BlockSpec(memory_space=s) for s in (pl.ANY, pltpu.VMEM))
    return pl.pallas_call(
        scatter_kernel,
        out_shape=jax.ShapeDtypeStruct((rows * tiles, LANES), F32),
        in_specs=[vmem, vmem, hbm, hbm],
        out_specs=hbm,
        scratch_shapes=[
            pltpu.VMEM((rows, rank), F32), pltpu.VMEM((rows, cols), F32), pltpu.VMEM((rows * tiles, LANES), F32),
            pltpu.VMEM((CHUNK * tiles, LANES), F32), pltpu.VMEM((CHUNK * tiles, LANES), F32),
            pltpu.VMEM((rank, cols), BF16), pltpu.VMEM((rank, cols), BF16),
            pltpu.VMEM(order.shape, I32), pltpu.SMEM(order.shape, I32),
            pltpu.SemaphoreType.DMA((2, rows // CHUNK)), pltpu.SemaphoreType.DMA, pltpu.SemaphoreType.DMA,
        ],
        compiler_params=pltpu.CompilerParams(vmem_limit_bytes=56 * MIB),
        name="far_scatter",
    )(order, down, basis, near)


def local(points_rhs, order, basis, near_blocks, near_pairs, transfer, coupling):
    rows, cols = points_rhs.shape
    tiles = cols // LANES
    levels = lax.axis_size("leaf").bit_length() - 1
    order = order.reshape(rows // LANES, LANES)
    x = points_rhs.reshape(rows // SUB, SUB, tiles, LANES).transpose(0, 2, 1, 3).reshape(rows * tiles, LANES)
    down, near = tree_call(levels, lax.axis_size("pts"), order, near_pairs.T, x, basis, near_blocks, transfer[0], coupling[0])
    out = scatter_call(order, down, basis, near)
    return out.reshape(rows // SUB, tiles, SUB, LANES).transpose(0, 2, 1, 3).reshape(rows, cols)


def solution(mesh):
    return jax.shard_map(
        local,
        mesh=mesh,
        in_specs=(
            P(("leaf", "pts"), None),
            P(("leaf", "pts"), None),
            P(("leaf", "pts"), None),
            P(("leaf", "pts"), None, None),
            P(("leaf", "pts"), None),
            P("leaf", None, None, None),
            P("leaf", None, None, None),
        ),
        out_specs=P(("leaf", "pts"), None),
        check_vma=False,
    )
```

profile of v0, /device:TPU:1, one launch (start us, length us, event | category | flops | bytes accessed | tf_op | source)
XLA Modules:
  0.0 70.4 jit_solution(11185794005907404804)
XLA Ops:
  0.0 56.1 %tree_near.1 = (f32[512,256]{1,0:T(8,128)}, f32[4096,512]{1,0:T(8,128)}) custom-call(s32[32,128]{1,0:T(8,128)} %bitcast.17, s32[2,64]{1,0:T(2,128)} %bitcast.19, f32[16384,128]{1,0:T(8,128)} %bitcast.14, f32[4096,256]{1,0:T(8,128)} %basis_hbm.3, f32[64,128,128]{2,1,0:T(8,128)} %blocks_hbm.1, f32[4,256,256]{2,1,0:T(8,128)} %bitcast.16, f32[5,256,256]{2,1,0:T(8,128)} %bitcast.15), custom_call_target="tpu_custom_call" | custom-call | tf_op jit(solution)/shard_map/tree_near/pallas_call | solution.py:306
  56.1 14.3 %far_scatter.1 = f32[16384,128]{1,0:T(8,128)} custom-call(s32[32,128]{1,0:T(8,128)} %bitcast.18, f32[512,256]{1,0:T(8,128)} %get-tuple-element.7.d_in, f32[4096,256]{1,0:T(8,128)} %basis_hbm.3, f32[4096,512]{1,0:T(8,128)} %get-tuple-element.8.near_hbm), custom_call_target="tpu_custom_call" | custom-call | tf_op jit(solution)/shard_map/far_scatter/pallas_call | solution.py:387
where the time goes:
time: 70.6 us; the launch traced here: 70.4 us
  Pallas kernels  70.3 us (100%)
    pallas_call x1, Pallas kernels, tree_call(): pl.pallas_call(functools.partial(tree_kernel, levels), out_shape=(shape((...  56.1 us
    pallas_call x1, Pallas kernels, scatter_call(): pl.pallas_call(scatter_kernel, out_shape=jax.ShapeDtypeStruct((rows * til...  14.3 us

commit v1 on v0

v1 whole, which is shorter than its diff:
```python
import functools

import jax
import jax.numpy as jnp
from jax import lax
from jax.experimental import pallas as pl
from jax.experimental.pallas import tpu as pltpu
from jax.sharding import PartitionSpec as P

MESH = pl.DeviceIdType.MESH
F32, BF16, I32 = jnp.float32, jnp.bfloat16, jnp.int32
LANES, SUB = 128, 8
MIB = 2**20
CHUNK = 256
HALVES = 2


def split(x):
    hi = x.astype(BF16)
    return hi, (x - hi.astype(F32)).astype(BF16)


def stack(x):
    return jnp.concatenate(split(x), axis=0)


def dot(a, b):
    return jnp.dot(a, b, preferred_element_type=F32)


def dot_t(a, b):
    return lax.dot_general(a, b, (((1,), (1,)), ((), ())), preferred_element_type=F32)


def three(mul, a, bh, bl):
    n = a.shape[0] // 2
    both = mul(a, bh)
    return both[:n] + (both[n:] + mul(a[:n], bl))


def row_address(order, tiles):
    return (order >> 3) * (SUB * tiles) + (order & (SUB - 1))


def tiles_of(ref, tiles, first, count):
    return [
        jnp.concatenate([ref[(g * tiles + j) * SUB:(g * tiles + j + 1) * SUB, :]
                         for g in range(first // SUB, (first + count) // SUB)], axis=0)
        for j in range(tiles)
    ]


def tree_kernel(levels, order_in, pairs_in, x_hbm, basis_hbm, blocks_hbm, t_hbm, g_hbm, d_out, nv, split_out,
                xv, bv, bt, rows_a, rows_b, acc, cin, edge, ph, pl_, blk, pre,
                tv, gv, tsib, wt, ws, wf, addr_v, addr, key_v, tab_v, tab,
                rs1, stage, rs2, cb, crecv, own, ebuf, dbuf, erecv,
                in_sem, t_send, t_recv, r_send, r_recv, c_send, c_recv, d_send, d_recv, e_send, e_recv):
    rows, cols = nv.shape
    rank = bv.shape[1]
    tiles = cols // LANES
    count, size = blk.shape[0], blk.shape[1]
    row_blocks = rows // size
    parts, half = cin.shape[1:3]
    chunks = rows // CHUNK
    leaf, p = lax.axis_index("leaf"), lax.axis_index("pts")
    top = levels - 1
    core, far_chip = (leaf, p ^ 1), (leaf, p ^ 2)
    following, before = (leaf, lax.rem(p + 1, parts)), (leaf, lax.rem(p + parts - 1, parts))
    siblings = [(leaf ^ (1 << l), p) for l in range(levels)]

    def load(src, dst, i):
        copy = pltpu.make_async_copy(src, dst, in_sem.at[i])
        copy.start()
        return copy

    def send(src, dst, to, send_sem, recv_sem):
        copy = pltpu.make_async_remote_copy(
            src_ref=src, dst_ref=dst, send_sem=send_sem, recv_sem=recv_sem, device_id=to, device_id_type=MESH)
        copy.start()
        return copy

    barrier = pltpu.get_barrier_semaphore()
    greeted = [core, far_chip, (leaf, p ^ 3)] + siblings
    for other in greeted:
        pl.semaphore_signal(barrier, inc=1, device_id=other, device_id_type=MESH)
    addr_v[...] = row_address(order_in[...], tiles)
    in_a = load(addr_v, addr, 5)
    in_x = load(x_hbm, xv, 3)
    in_b = load(basis_hbm, bv, 2)
    in_t = load(t_hbm, tv, 0)
    in_g = load(g_hbm, gv, 1)
    in_k = load(blocks_hbm, blk, 4)

    key_v[...] = jnp.full(key_v.shape, 1e6, F32)
    key_v[0:1, :count] = (2 * pairs_in[0:1, :] + pairs_in[1:2, :]).astype(F32)
    across = jnp.broadcast_to(key_v[0:1, :], (LANES, LANES))
    down_key = across.T
    row_i = lax.broadcasted_iota(I32, (LANES, LANES), 0)
    col_i = lax.broadcasted_iota(I32, (LANES, LANES), 1)
    col_f = col_i.astype(F32)
    one = lambda cond: jnp.where(cond, 1.0, 0.0)
    twin = one((across == down_key) & (col_i < row_i))
    place = jnp.sum(twin + one(across < down_key), axis=1, keepdims=True)
    hit = one(place == col_f)
    again = jnp.where(jnp.sum(twin, axis=1, keepdims=True) > 0, 1.0, 0.0)
    total = lambda x: jnp.sum(x, axis=0, keepdims=True)
    found = total(one(down_key == col_f))
    last = jnp.where(found > 0, total(one(down_key <= col_f)) - 1.0, float(count))
    tab_v[...] = jnp.zeros_like(tab_v)
    tab_v[0:1, :] = total(hit * row_i.astype(F32)).astype(I32)
    tab_v[1:2, :] = total(hit * again).astype(I32)
    tab_v[2:3, :] = last.astype(I32)
    in_tab = load(tab_v, tab, 6)
    pre[0] = jnp.zeros((size, size), F32)
    pre[count] = jnp.zeros((size, size), F32)
    in_a.wait()
    in_tab.wait()
    in_x.wait()

    def gather(i, buf):
        step = 32
        for g in range(CHUNK // step):
            ids = [g * step + u for u in range(step)]
            vals = [xv[pl.ds(addr[i * (CHUNK // LANES) + k // LANES, k % LANES], tiles, stride=SUB), :] for k in ids]
            for k, val in zip(ids, vals):
                buf[pl.ds((k // SUB) * (SUB * tiles) + k % SUB, tiles, stride=SUB), :] = val

    def keep(i, buf):
        to = pl.ds(pl.multiple_of(size + i * CHUNK, size), CHUNK)
        for j, part in enumerate(tiles_of(buf, tiles, 0, CHUNK)):
            ph[to, j * LANES:(j + 1) * LANES], pl_[to, j * LANES:(j + 1) * LANES] = split(part)

    gather(0, rows_a)
    pl.semaphore_wait(barrier, len(greeted))
    moved = [send(t_hbm.at[l], tsib.at[l], siblings[l], t_send.at[l], t_recv.at[l]) for l in range(top)]
    for j, part in enumerate(tiles_of(rows_a, tiles, 0, size)):
        edge[0, :, j * LANES:(j + 1) * LANES] = part

    @pl.loop(0, chunks // 2 - 1)
    def _(i):
        gather(2 * i + 1, rows_b)
        keep(2 * i, rows_a)
        gather(2 * i + 2, rows_a)
        keep(2 * i + 1, rows_b)

    gather(chunks - 1, rows_b)
    keep(chunks - 2, rows_a)
    for j, part in enumerate(tiles_of(rows_b, tiles, CHUNK - size, size)):
        edge[1, :, j * LANES:(j + 1) * LANES] = part
    keep(chunks - 1, rows_b)
    in_b.wait()

    @pl.loop(0, chunks)
    def _(i):
        at = pl.multiple_of(i * CHUNK, CHUNK)
        bt[:, pl.ds(at, CHUNK)] = stack(bv[pl.ds(at, CHUNK), :].T)

    span = cols // HALVES

    def compress(h, first, last):
        deep = min(1024, rows)

        @pl.loop(first * rows // deep // 2, last * rows // deep // 2)
        def _(i):
            at = pl.multiple_of(i * deep, deep)
            to = pl.ds(pl.multiple_of(size + at, size), deep)
            part = three(dot, bt[:, pl.ds(at, deep)], ph[to, h * span:(h + 1) * span], pl_[to, h * span:(h + 1) * span])
            acc[...] = jnp.where(i == 0, part, acc[...] + part)

        if last == 2:
            for q in range(span // LANES):
                turned = acc[:, q * LANES:(q + 1) * LANES].T
                for k in range(LANES // half):
                    cin[h, q * (LANES // half) + k] = turned[k * half:(k + 1) * half]

    hs = [pl.ds(h * half, half) for h in range(HALVES)]
    to_core = [[], []]
    to_far = []

    def sum_core(h):
        for k in range(2):
            to_core[k].append(send(cin.at[h, p ^ (3 - 2 * k)], rs1.at[k, hs[h]], core, r_send.at[k, h], r_recv.at[k, h]))

    def sum_far(h):
        to_core[0][h].wait_recv()
        stage[hs[h], :] = cin[h, p ^ 2] + rs1[0, hs[h], :]
        to_far.append(send(stage.at[hs[h]], rs2.at[hs[h]], far_chip, r_send.at[2, h], r_recv.at[2, h]))

    acc[...] = jnp.zeros_like(acc)
    compress(0, 0, 2)
    sum_core(0)
    for h in range(1, HALVES):
        compress(h, 0, 1)
        sum_far(h - 1)
        compress(h, 1, 2)
        sum_core(h)
    sum_far(HALVES - 1)
    for copy in to_core[1]:
        copy.wait_recv()
    sent = to_core[0] + to_core[1] + to_far + moved

    in_t.wait()
    in_g.wait()
    for l in range(top):
        wt[l, 0], wt[l, 1] = split(tv[l])
    wf[...] = tv[0]
    ws[0, 0], ws[0, 1] = split(gv[0])
    for l in range(1, levels):
        path = stack(wf[...])
        gh, gl = split(gv[l])
        ws[l, 0], ws[l, 1] = split(three(dot, path, gh, gl))
        if l < top:
            wf[...] = three(dot, path, wt[l, 0], wt[l, 1])

    in_k.wait()

    @pl.loop(0, count)
    def _(m):
        pre[m] = jnp.where(tab[1, m] > 0, pre[jnp.maximum(m - 1, 0)], 0.0) + blk[jnp.clip(tab[0, m], 0, count - 1)]

    def near(first, number):
        if not number:
            return

        @pl.loop(first, first + number)
        def _(u):
            none = jnp.zeros((size, size), F32)
            get = lambda r, o: pre[jnp.clip(tab[2, 6 * u + 3 * r + o], 0, count)]
            upper = jnp.concatenate([get(0, 0), get(0, 1), get(0, 2), none], axis=1)
            lower = jnp.concatenate([none, get(1, 0), get(1, 1), get(1, 2)], axis=1)
            band = stack(jnp.concatenate([upper, lower], axis=0))
            at = pl.multiple_of(u * (2 * size), 2 * size)
            span = pl.ds(at, 4 * size)
            nv[pl.ds(at, 2 * size), :] = three(dot, band, ph[span, :], pl_[span, :])

    units = row_blocks // 2
    inner = units - 2
    cuts = [1 + inner * i // (levels + 1) for i in range(levels + 2)]

    def near_step(i):
        near(cuts[i], cuts[i + 1] - cuts[i])

    near_step(0)
    for l in range(top):
        moved[l].wait_recv()
        wt[top + l, 0], wt[top + l, 1] = split(tsib[l])

    edges = []
    up = []
    for h in range(HALVES):
        to_far[h].wait_recv()
        cb[0, hs[h], :] = cin[h, p] + (rs1[1, hs[h], :] + rs2[hs[h], :])
        up.append(send(cb.at[0, hs[h]], crecv.at[0, hs[h]], siblings[0], c_send.at[0, h], c_recv.at[0, h]))
    for l in range(top):
        if l == 0:
            edges.append(send(edge.at[1], erecv.at[0], following, e_send.at[0], e_recv.at[0]))
            edges.append(send(edge.at[0], erecv.at[1], before, e_send.at[1], e_recv.at[1]))
        own[...] = three(dot, stack(cb[l]), wt[l, 0], wt[l, 1])
        near_step(1 + l)
        for h in range(HALVES):
            up[l * HALVES + h].wait_recv()
            cb[l + 1, hs[h], :] = own[hs[h], :] + three(dot, stack(crecv[l, hs[h], :]), wt[top + l, 0], wt[top + l, 1])
            up.append(send(cb.at[l + 1, hs[h]], crecv.at[l + 1, hs[h]], siblings[l + 1], c_send.at[l + 1, h], c_recv.at[l + 1, h]))
        part = three(dot_t, stack(crecv[l]), ws[l, 0], ws[l, 1])
        ebuf[...] = part if l == 0 else ebuf[...] + part
    near_step(levels)

    @pl.loop(0, chunks)
    def _(i):
        at = pl.multiple_of(i * CHUNK, CHUNK)
        split_out[pl.ds(2 * at, 2 * CHUNK), :] = stack(bv[pl.ds(at, CHUNK), :])

    d0, d1, d2 = [], [], []
    for h in range(HALVES):
        up[top * HALVES + h].wait_recv()
        dbuf[h, p] = ebuf[hs[h], :] + three(dot_t, stack(crecv[top, hs[h], :]), ws[top, 0], ws[top, 1])
        mine = dbuf.at[h, p]
        d0.append(send(mine, mine, far_chip, d_send.at[0, h], d_recv.at[0, h]))
        d1.append(send(mine, mine, core, d_send.at[1, h], d_recv.at[1, h]))

    for copy in edges:
        copy.wait_recv()
    ph[:size, :], pl_[:size, :] = split(jnp.where(p == 0, 0.0, erecv[0]))
    ph[size + rows:, :], pl_[size + rows:, :] = split(jnp.where(p == parts - 1, 0.0, erecv[1]))
    near(0, 1)
    near(units - 1, 1)
    for h in range(HALVES):
        d0[h].wait_recv()
        other = dbuf.at[h, p ^ 2]
        d2.append(send(other, other, core, d_send.at[2, h], d_recv.at[2, h]))
    for copy in d1 + d2:
        copy.wait_recv()
    for h in range(HALVES):
        for q in range(parts):
            at = (h * parts + q) * half
            d_out[at:at + half, :] = dbuf[h, q]
    for copy in sent + up + edges + d0 + d1 + d2:
        copy.wait_send()


def tree_call(levels, parts, order, pairs, x, basis, blocks, transfer, coupling):
    rows, rank = basis.shape
    tiles = x.shape[0] // rows
    cols = tiles * LANES
    count, size = blocks.shape[0], blocks.shape[1]
    width = cols // parts
    hbm, vmem = (pl.BlockSpec(memory_space=s) for s in (pl.ANY, pltpu.VMEM))
    shape = jax.ShapeDtypeStruct
    dma = pltpu.SemaphoreType.DMA
    part = (width, rank)
    by_half = (HALVES, parts, width // HALVES, rank)
    padded = (rows + 2 * size, cols)
    scratch = [
        (x.shape, F32), (basis.shape, F32), ((2 * rank, rows), BF16), ((CHUNK * tiles, LANES), F32), ((CHUNK * tiles, LANES), F32),
        ((rank, cols // HALVES), F32), (by_half, F32), ((2, size, cols), F32), (padded, BF16), (padded, BF16),
        (blocks.shape, F32), ((count + 1, size, size), F32),
        (transfer.shape, F32), (coupling.shape, F32), (transfer.shape, F32),
        ((2 * (levels - 1), 2, rank, rank), BF16), ((levels, 2, rank, rank), BF16), ((rank, rank), F32),
        (order.shape, I32), None, ((SUB, LANES), F32), ((SUB, LANES), I32), None,
        ((2,) + part, F32), (part, F32), (part, F32), ((levels,) + part, F32), ((levels,) + part, F32),
        (part, F32), (part, F32), (by_half, F32), ((2, size, cols), F32),
    ]
    scratch = [pltpu.VMEM(*s) if s else None for s in scratch]
    scratch[19] = pltpu.SMEM(order.shape, I32)
    scratch[22] = pltpu.SMEM((SUB, LANES), I32)
    return pl.pallas_call(
        functools.partial(tree_kernel, levels),
        out_shape=(pltpu.VMEM((cols, rank), F32), pltpu.VMEM((rows, cols), F32), pltpu.VMEM((2 * rows, rank), BF16)),
        in_specs=[vmem, vmem, hbm, hbm, hbm, hbm, hbm],
        out_specs=(vmem, vmem, vmem),
        scratch_shapes=scratch + [
            dma((7,)), dma((levels - 1,)), dma((levels - 1,)), dma((3, HALVES)), dma((3, HALVES)),
            dma((levels, HALVES)), dma((levels, HALVES)), dma((3, HALVES)), dma((3, HALVES)), dma((2,)), dma((2,)),
        ],
        compiler_params=pltpu.CompilerParams(vmem_limit_bytes=48 * MIB, collective_id=0, has_side_effects=True),
        name="tree_near",
    )(order, pairs, x, basis, blocks, transfer, coupling)


def scatter_kernel(order_in, d_in, basis, near, out_hbm, ov, rows_a, rows_b, dh, dl, addr_v, addr, a_sem, out_sem):
    rows, cols = near.shape
    tiles = cols // LANES
    chunks = rows // CHUNK
    addr_v[...] = row_address(order_in[...], tiles)
    in_a = pltpu.make_async_copy(addr_v, addr, a_sem)
    in_a.start()
    for j in range(tiles):
        h, l = split(d_in[j * LANES:(j + 1) * LANES, :].T)
        dh[:, j * LANES:(j + 1) * LANES] = h
        dl[:, j * LANES:(j + 1) * LANES] = l
    in_a.wait()

    def multiply(i, buf):
        at = pl.multiple_of(i * CHUNK, CHUNK)
        total = near[pl.ds(at, CHUNK), :] + three(dot, basis[pl.ds(2 * at, 2 * CHUNK), :], dh[...], dl[...])
        for g in range(CHUNK // SUB):
            for j in range(tiles):
                buf[(g * tiles + j) * SUB:(g * tiles + j + 1) * SUB, :] = total[g * SUB:(g + 1) * SUB, j * LANES:(j + 1) * LANES]

    def scatter(i, buf):
        for k in range(CHUNK):
            to = addr[i * (CHUNK // LANES) + k // LANES, k % LANES]
            ov[pl.ds(to, tiles, stride=SUB), :] = buf[pl.ds((k // SUB) * (SUB * tiles) + k % SUB, tiles, stride=SUB), :]

    multiply(0, rows_a)

    @pl.loop(0, chunks // 2 - 1)
    def _(i):
        multiply(2 * i + 1, rows_b)
        scatter(2 * i, rows_a)
        multiply(2 * i + 2, rows_a)
        scatter(2 * i + 1, rows_b)

    multiply(chunks - 1, rows_b)
    scatter(chunks - 2, rows_a)
    scatter(chunks - 1, rows_b)
    out = pltpu.make_async_copy(ov, out_hbm, out_sem)
    out.start()
    out.wait()


def scatter_call(order, down, basis, near):
    rows, cols = near.shape
    rank = basis.shape[1]
    tiles = cols // LANES
    hbm, vmem = (pl.BlockSpec(memory_space=s) for s in (pl.ANY, pltpu.VMEM))
    return pl.pallas_call(
        scatter_kernel,
        out_shape=jax.ShapeDtypeStruct((rows * tiles, LANES), F32),
        in_specs=[vmem, vmem, vmem, vmem],
        out_specs=hbm,
        scratch_shapes=[
            pltpu.VMEM((rows * tiles, LANES), F32),
            pltpu.VMEM((CHUNK * tiles, LANES), F32), pltpu.VMEM((CHUNK * tiles, LANES), F32),
            pltpu.VMEM((rank, cols), BF16), pltpu.VMEM((rank, cols), BF16),
            pltpu.VMEM(order.shape, I32), pltpu.SMEM(order.shape, I32),
            pltpu.SemaphoreType.DMA, pltpu.SemaphoreType.DMA,
        ],
        compiler_params=pltpu.CompilerParams(vmem_limit_bytes=24 * MIB),
        name="far_scatter",
    )(order, down, basis, near)


def local(points_rhs, order, basis, near_blocks, near_pairs, transfer, coupling):
    rows, cols = points_rhs.shape
    tiles = cols // LANES
    levels = lax.axis_size("leaf").bit_length() - 1
    order = order.reshape(rows // LANES, LANES)
    x = points_rhs.reshape(rows // SUB, SUB, tiles, LANES).transpose(0, 2, 1, 3).reshape(rows * tiles, LANES)
    down, near, halves = tree_call(levels, lax.axis_size("pts"), order, near_pairs.T, x, basis, near_blocks, transfer[0], coupling[0])
    out = scatter_call(order, *(pltpu.with_memory_space_constraint(v, pltpu.VMEM) for v in (down, halves, near)))
    return out.reshape(rows // SUB, tiles, SUB, LANES).transpose(0, 2, 1, 3).reshape(rows, cols)


def solution(mesh):
    return jax.shard_map(
        local,
        mesh=mesh,
        in_specs=(
            P(("leaf", "pts"), None),
            P(("leaf", "pts"), None),
            P(("leaf", "pts"), None),
            P(("leaf", "pts"), None, None),
            P(("leaf", "pts"), None),
            P("leaf", None, None, None),
            P("leaf", None, None, None),
        ),
        out_specs=P(("leaf", "pts"), None),
        check_vma=False,
    )
```

time: 70.6 us -> 67.5 us (0.956)
  Pallas kernels: 70.3 us -> 67.4 us
    pallas_call x1, Pallas kernels: 14.3 us -> 10.4 us  [scatter_call(): pl.pallas_call(scatter_kernel, out_shape=jax.ShapeDtypeStruct((rows * til...]
    pallas_call x1, Pallas kernels: 56.1 us -> 57 us  [tree_call(): pl.pallas_call(functools.partial(tree_kernel, levels), out_shape=(pltpu.V...]
where the time goes in v1:
time: 67.5 us; the launch traced here: 67.4 us
  Pallas kernels  67.4 us (100%)
    pallas_call x1, Pallas kernels, tree_call(): pl.pallas_call(functools.partial(tree_kernel, levels), out_shape=(pltpu.V...  57 us
    pallas_call x1, Pallas kernels, scatter_call(): pl.pallas_call(scatter_kernel, out_shape=jax.ShapeDtypeStruct((rows * til...  10.4 us

profile of v1, /device:TPU:1, one launch (start us, length us, event | category | flops | bytes accessed | tf_op | source)
XLA Modules:
  0.0 67.4 jit_solution(4202377429021180426)
XLA Ops:
  0.0 0.0 copy-start
  0.0 57.0 %tree_near.1 = (f32[512,256]{1,0:T(8,128)S(1)}, f32[4096,512]{1,0:T(8,128)S(1)}, bf16[8192,256]{1,0:T(8,128)(2,1)S(1)}) custom-call(s32[32,128]{1,0:T(8,128)} %bitcast.14, s32[2,64]{1,0:T(2,128)} %bitcast.19, f32[16384,128]{1,0:T(8,128)} %bitcast.16, f32[4096,256]{1,0:T(8,128)} %basis_hbm.1, f32[64,128,128]{2,1,0:T(8,128)} %blocks_hbm.1, ...), custom_call_target="tpu_custom_call" | custom-call | tf_op jit(solution)/shard_map/tree_near/pallas_call | solution.py:326
  57.0 0.0 copy-done
  57.0 10.4 %far_scatter.1 = f32[16384,128]{1,0:T(8,128)} custom-call(s32[32,128]{1,0:T(8,128)S(1)} %bitcast.15, f32[512,256]{1,0:T(8,128)S(1)} %get-tuple-element.8.d_in, bf16[8192,256]{1,0:T(8,128)(2,1)S(1)} %get-tuple-element.9.basis, f32[4096,512]{1,0:T(8,128)S(1)} %get-tuple-element.10.near), custom_call_target="tpu_custom_call" | custom-call | tf_op jit(solution)/shard_map/far_scatter/pallas_call | solution.py:387
Async XLA Ops:
  0.0 57.0 %copy-start = (s32[1,4096]{1,0:T(1,128)S(1)}, s32[1,4096]{1,0:T(1,128)}, u32[]{:S(2)}) copy-start(s32[1,4096]{1,0:T(1,128)} %param.8) | copy-start | bytes 49156

commit v2 on v1

--- a/solution.py
+++ b/solution.py
@@ -12,7 +12,7 @@
 LANES, SUB = 128, 8
 MIB = 2**20
 CHUNK = 256
-HALVES = 2
+PIECES = 4
 
 
 def split(x):
@@ -60,7 +60,8 @@
     tiles = cols // LANES
     count, size = blk.shape[0], blk.shape[1]
     row_blocks = rows // size
-    parts, half = cin.shape[1:3]
+    parts, width = cin.shape[:2]
+    piece = width // PIECES
     chunks = rows // CHUNK
     leaf, p = lax.axis_index("leaf"), lax.axis_index("pts")
     top = levels - 1
@@ -85,8 +86,8 @@
         pl.semaphore_signal(barrier, inc=1, device_id=other, device_id_type=MESH)
     addr_v[...] = row_address(order_in[...], tiles)
     in_a = load(addr_v, addr, 5)
+    in_b = load(basis_hbm, bv, 2)
     in_x = load(x_hbm, xv, 3)
-    in_b = load(basis_hbm, bv, 2)
     in_t = load(t_hbm, tv, 0)
     in_g = load(g_hbm, gv, 1)
     in_k = load(blocks_hbm, blk, 4)
@@ -113,6 +114,14 @@
     in_tab = load(tab_v, tab, 6)
     pre[0] = jnp.zeros((size, size), F32)
     pre[count] = jnp.zeros((size, size), F32)
+    acc[...] = jnp.zeros_like(acc)
+    in_b.wait()
+
+    @pl.loop(0, chunks)
+    def _(i):
+        at = pl.multiple_of(i * CHUNK, CHUNK)
+        bt[:, pl.ds(at, CHUNK)] = stack(bv[pl.ds(at, CHUNK), :].T)
+
     in_a.wait()
     in_tab.wait()
     in_x.wait()
@@ -125,10 +134,14 @@
             for k, val in zip(ids, vals):
                 buf[pl.ds((k // SUB) * (SUB * tiles) + k % SUB, tiles, stride=SUB), :] = val
 
-    def keep(i, buf):
-        to = pl.ds(pl.multiple_of(size + i * CHUNK, size), CHUNK)
-        for j, part in enumerate(tiles_of(buf, tiles, 0, CHUNK)):
-            ph[to, j * LANES:(j + 1) * LANES], pl_[to, j * LANES:(j + 1) * LANES] = split(part)
+    def compress(i, buf):
+        at = pl.multiple_of(i * CHUNK, CHUNK)
+        hi, lo = zip(*[split(part) for part in tiles_of(buf, tiles, 0, CHUNK)])
+        hi, lo = jnp.concatenate(hi, axis=1), jnp.concatenate(lo, axis=1)
+        to = pl.ds(pl.multiple_of(size + at, size), CHUNK)
+        ph[to, :] = hi
+        pl_[to, :] = lo
+        acc[...] += three(dot, bt[:, pl.ds(at, CHUNK)], hi, lo)
 
     gather(0, rows_a)
     pl.semaphore_wait(barrier, len(greeted))
@@ -139,62 +152,26 @@
     @pl.loop(0, chunks // 2 - 1)
     def _(i):
         gather(2 * i + 1, rows_b)
-        keep(2 * i, rows_a)
+        compress(2 * i, rows_a)
         gather(2 * i + 2, rows_a)
-        keep(2 * i + 1, rows_b)
+        compress(2 * i + 1, rows_b)
 
     gather(chunks - 1, rows_b)
-    keep(chunks - 2, rows_a)
+    compress(chunks - 2, rows_a)
     for j, part in enumerate(tiles_of(rows_b, tiles, CHUNK - size, size)):
         edge[1, :, j * LANES:(j + 1) * LANES] = part
-    keep(chunks - 1, rows_b)
-    in_b.wait()
-
-    @pl.loop(0, chunks)
-    def _(i):
-        at = pl.multiple_of(i * CHUNK, CHUNK)
-        bt[:, pl.ds(at, CHUNK)] = stack(bv[pl.ds(at, CHUNK), :].T)
-
-    span = cols // HALVES
-
-    def compress(h, first, last):
-        deep = min(1024, rows)
-
-        @pl.loop(first * rows // deep // 2, last * rows // deep // 2)
-        def _(i):
-            at = pl.multiple_of(i * deep, deep)
-            to = pl.ds(pl.multiple_of(size + at, size), deep)
-            part = three(dot, bt[:, pl.ds(at, deep)], ph[to, h * span:(h + 1) * span], pl_[to, h * span:(h + 1) * span])
-            acc[...] = jnp.where(i == 0, part, acc[...] + part)
-
-        if last == 2:
-            for q in range(span // LANES):
-                turned = acc[:, q * LANES:(q + 1) * LANES].T
-                for k in range(LANES // half):
-                    cin[h, q * (LANES // half) + k] = turned[k * half:(k + 1) * half]
-
-    hs = [pl.ds(h * half, half) for h in range(HALVES)]
-    to_core = [[], []]
+    compress(chunks - 1, rows_b)
+
+    hs = [pl.ds(h * piece, piece) for h in range(PIECES)]
+    for q in range(parts):
+        cin[q] = acc[:, q * width:(q + 1) * width].T
+    to_core = [[send(cin.at[p ^ (3 - 2 * k), hs[h]], rs1.at[k, hs[h]], core, r_send.at[k, h], r_recv.at[k, h])
+                for h in range(PIECES)] for k in range(2)]
     to_far = []
-
-    def sum_core(h):
-        for k in range(2):
-            to_core[k].append(send(cin.at[h, p ^ (3 - 2 * k)], rs1.at[k, hs[h]], core, r_send.at[k, h], r_recv.at[k, h]))
-
-    def sum_far(h):
+    for h in range(PIECES):
         to_core[0][h].wait_recv()
-        stage[hs[h], :] = cin[h, p ^ 2] + rs1[0, hs[h], :]
+        stage[hs[h], :] = cin[p ^ 2, hs[h], :] + rs1[0, hs[h], :]
         to_far.append(send(stage.at[hs[h]], rs2.at[hs[h]], far_chip, r_send.at[2, h], r_recv.at[2, h]))
-
-    acc[...] = jnp.zeros_like(acc)
-    compress(0, 0, 2)
-    sum_core(0)
-    for h in range(1, HALVES):
-        compress(h, 0, 1)
-        sum_far(h - 1)
-        compress(h, 1, 2)
-        sum_core(h)
-    sum_far(HALVES - 1)
     for copy in to_core[1]:
         copy.wait_recv()
     sent = to_core[0] + to_core[1] + to_far + moved
@@ -204,10 +181,13 @@
     for l in range(top):
         wt[l, 0], wt[l, 1] = split(tv[l])
     wf[...] = tv[0]
-    ws[0, 0], ws[0, 1] = split(gv[0])
-    for l in range(1, levels):
+
+    def weight(l):
+        gh, gl = split(gv[l])
+        if l == 0:
+            ws[l, 0], ws[l, 1] = gh, gl
+            return
         path = stack(wf[...])
-        gh, gl = split(gv[l])
         ws[l, 0], ws[l, 1] = split(three(dot, path, gh, gl))
         if l < top:
             wf[...] = three(dot, path, wt[l, 0], wt[l, 1])
@@ -235,46 +215,48 @@
 
     units = row_blocks // 2
     inner = units - 2
-    cuts = [1 + inner * i // (levels + 1) for i in range(levels + 2)]
+    cuts = [1 + inner * i // (levels + 2) for i in range(levels + 3)]
 
     def near_step(i):
         near(cuts[i], cuts[i + 1] - cuts[i])
 
     near_step(0)
+
+    @pl.loop(0, chunks)
+    def _(i):
+        at = pl.multiple_of(i * CHUNK, CHUNK)
+        split_out[pl.ds(2 * at, 2 * CHUNK), :] = stack(bv[pl.ds(at, CHUNK), :])
+
     for l in range(top):
         moved[l].wait_recv()
         wt[top + l, 0], wt[top + l, 1] = split(tsib[l])
 
     edges = []
     up = []
-    for h in range(HALVES):
+    for h in range(PIECES):
         to_far[h].wait_recv()
-        cb[0, hs[h], :] = cin[h, p] + (rs1[1, hs[h], :] + rs2[hs[h], :])
+        cb[0, hs[h], :] = cin[p, hs[h], :] + (rs1[1, hs[h], :] + rs2[hs[h], :])
         up.append(send(cb.at[0, hs[h]], crecv.at[0, hs[h]], siblings[0], c_send.at[0, h], c_recv.at[0, h]))
     for l in range(top):
         if l == 0:
             edges.append(send(edge.at[1], erecv.at[0], following, e_send.at[0], e_recv.at[0]))
             edges.append(send(edge.at[0], erecv.at[1], before, e_send.at[1], e_recv.at[1]))
         own[...] = three(dot, stack(cb[l]), wt[l, 0], wt[l, 1])
+        weight(l)
         near_step(1 + l)
-        for h in range(HALVES):
-            up[l * HALVES + h].wait_recv()
+        for h in range(PIECES):
+            up[l * PIECES + h].wait_recv()
             cb[l + 1, hs[h], :] = own[hs[h], :] + three(dot, stack(crecv[l, hs[h], :]), wt[top + l, 0], wt[top + l, 1])
             up.append(send(cb.at[l + 1, hs[h]], crecv.at[l + 1, hs[h]], siblings[l + 1], c_send.at[l + 1, h], c_recv.at[l + 1, h]))
         part = three(dot_t, stack(crecv[l]), ws[l, 0], ws[l, 1])
         ebuf[...] = part if l == 0 else ebuf[...] + part
+    weight(top)
     near_step(levels)
-
-    @pl.loop(0, chunks)
-    def _(i):
-        at = pl.multiple_of(i * CHUNK, CHUNK)
-        split_out[pl.ds(2 * at, 2 * CHUNK), :] = stack(bv[pl.ds(at, CHUNK), :])
-
     d0, d1, d2 = [], [], []
-    for h in range(HALVES):
-        up[top * HALVES + h].wait_recv()
-        dbuf[h, p] = ebuf[hs[h], :] + three(dot_t, stack(crecv[top, hs[h], :]), ws[top, 0], ws[top, 1])
-        mine = dbuf.at[h, p]
+    for h in range(PIECES):
+        up[top * PIECES + h].wait_recv()
+        dbuf[p, hs[h], :] = ebuf[hs[h], :] + three(dot_t, stack(crecv[top, hs[h], :]), ws[top, 0], ws[top, 1])
+        mine = dbuf.at[p, hs[h]]
         d0.append(send(mine, mine, far_chip, d_send.at[0, h], d_recv.at[0, h]))
         d1.append(send(mine, mine, core, d_send.at[1, h], d_recv.at[1, h]))
 
@@ -283,17 +265,16 @@
     ph[:size, :], pl_[:size, :] = split(jnp.where(p == 0, 0.0, erecv[0]))
     ph[size + rows:, :], pl_[size + rows:, :] = split(jnp.where(p == parts - 1, 0.0, erecv[1]))
     near(0, 1)
+    near_step(levels + 1)
     near(units - 1, 1)
-    for h in range(HALVES):
+    for h in range(PIECES):
         d0[h].wait_recv()
-        other = dbuf.at[h, p ^ 2]
+        other = dbuf.at[p ^ 2, hs[h]]
         d2.append(send(other, other, core, d_send.at[2, h], d_recv.at[2, h]))
     for copy in d1 + d2:
         copy.wait_recv()
-    for h in range(HALVES):
-        for q in range(parts):
-            at = (h * parts + q) * half
-            d_out[at:at + half, :] = dbuf[h, q]
+    for q in range(parts):
+        d_out[q * width:(q + 1) * width, :] = dbuf[q]
     for copy in sent + up + edges + d0 + d1 + d2:
         copy.wait_send()
 
@@ -308,17 +289,16 @@
     shape = jax.ShapeDtypeStruct
     dma = pltpu.SemaphoreType.DMA
     part = (width, rank)
-    by_half = (HALVES, parts, width // HALVES, rank)
     padded = (rows + 2 * size, cols)
     scratch = [
         (x.shape, F32), (basis.shape, F32), ((2 * rank, rows), BF16), ((CHUNK * tiles, LANES), F32), ((CHUNK * tiles, LANES), F32),
-        ((rank, cols // HALVES), F32), (by_half, F32), ((2, size, cols), F32), (padded, BF16), (padded, BF16),
+        ((rank, cols), F32), ((parts,) + part, F32), ((2, size, cols), F32), (padded, BF16), (padded, BF16),
         (blocks.shape, F32), ((count + 1, size, size), F32),
         (transfer.shape, F32), (coupling.shape, F32), (transfer.shape, F32),
         ((2 * (levels - 1), 2, rank, rank), BF16), ((levels, 2, rank, rank), BF16), ((rank, rank), F32),
         (order.shape, I32), None, ((SUB, LANES), F32), ((SUB, LANES), I32), None,
         ((2,) + part, F32), (part, F32), (part, F32), ((levels,) + part, F32), ((levels,) + part, F32),
-        (part, F32), (part, F32), (by_half, F32), ((2, size, cols), F32),
+        (part, F32), (part, F32), ((parts,) + part, F32), ((2, size, cols), F32),
     ]
     scratch = [pltpu.VMEM(*s) if s else None for s in scratch]
     scratch[19] = pltpu.SMEM(order.shape, I32)
@@ -329,8 +309,8 @@
         in_specs=[vmem, vmem, hbm, hbm, hbm, hbm, hbm],
         out_specs=(vmem, vmem, vmem),
         scratch_shapes=scratch + [
-            dma((7,)), dma((levels - 1,)), dma((levels - 1,)), dma((3, HALVES)), dma((3, HALVES)),
-            dma((levels, HALVES)), dma((levels, HALVES)), dma((3, HALVES)), dma((3, HALVES)), dma((2,)), dma((2,)),
+            dma((7,)), dma((levels - 1,)), dma((levels - 1,)), dma((3, PIECES)), dma((3, PIECES)),
+            dma((levels, PIECES)), dma((levels, PIECES)), dma((3, PIECES)), dma((3, PIECES)), dma((2,)), dma((2,)),
         ],
         compiler_params=pltpu.CompilerParams(vmem_limit_bytes=48 * MIB, collective_id=0, has_side_effects=True),
         name="tree_near",

time: 67.5 us -> 62.6 us (0.927)
  Pallas kernels: 67.4 us -> 62.4 us
    pallas_call x1, Pallas kernels: 57 us -> 52 us  [tree_call(): pl.pallas_call(functools.partial(tree_kernel, levels), out_shape=(pltpu.V...]
where the time goes in v2:
time: 62.6 us; the launch traced here: 62.4 us
  Pallas kernels  62.4 us (100%)
    pallas_call x1, Pallas kernels, tree_call(): pl.pallas_call(functools.partial(tree_kernel, levels), out_shape=(pltpu.V...  52 us
    pallas_call x1, Pallas kernels, scatter_call(): pl.pallas_call(scatter_kernel, out_shape=jax.ShapeDtypeStruct((rows * til...  10.4 us

profile of v2, /device:TPU:1, one launch (start us, length us, event | category | flops | bytes accessed | tf_op | source)
XLA Modules:
  0.0 62.4 jit_solution(4080631273166387496)
XLA Ops:
  0.0 0.0 copy-start
  0.0 52.0 %tree_near.1 = (f32[512,256]{1,0:T(8,128)S(1)}, f32[4096,512]{1,0:T(8,128)S(1)}, bf16[8192,256]{1,0:T(8,128)(2,1)S(1)}) custom-call(s32[32,128]{1,0:T(8,128)} %bitcast.14, s32[2,64]{1,0:T(2,128)} %bitcast.19, f32[16384,128]{1,0:T(8,128)} %bitcast.16, f32[4096,256]{1,0:T(8,128)} %basis_hbm.1, f32[64,128,128]{2,1,0:T(8,128)} %blocks_hbm.1, ...), custom_call_target="tpu_custom_call" | custom-call | tf_op jit(solution)/shard_map/tree_near/pallas_call | solution.py:306
  52.0 0.0 copy-done
  52.0 10.4 %far_scatter.1 = f32[16384,128]{1,0:T(8,128)} custom-call(s32[32,128]{1,0:T(8,128)S(1)} %bitcast.15, f32[512,256]{1,0:T(8,128)S(1)} %get-tuple-element.8.d_in, bf16[8192,256]{1,0:T(8,128)(2,1)S(1)} %get-tuple-element.9.basis, f32[4096,512]{1,0:T(8,128)S(1)} %get-tuple-element.10.near), custom_call_target="tpu_custom_call" | custom-call | tf_op jit(solution)/shard_map/far_scatter/pallas_call | solution.py:367
Async XLA Ops:
  0.0 52.0 %copy-start = (s32[1,4096]{1,0:T(1,128)S(1)}, s32[1,4096]{1,0:T(1,128)}, u32[]{:S(2)}) copy-start(s32[1,4096]{1,0:T(1,128)} %param.8) | copy-start | bytes 49156

commit v3 on v2

--- a/solution.py
+++ b/solution.py
@@ -53,8 +53,8 @@
 def tree_kernel(levels, order_in, pairs_in, x_hbm, basis_hbm, blocks_hbm, t_hbm, g_hbm, d_out, nv, split_out,
                 xv, bv, bt, rows_a, rows_b, acc, cin, edge, ph, pl_, blk, pre,
                 tv, gv, tsib, wt, ws, wf, addr_v, addr, key_v, tab_v, tab,
-                rs1, stage, rs2, cb, crecv, own, ebuf, dbuf, erecv,
-                in_sem, t_send, t_recv, r_send, r_recv, c_send, c_recv, d_send, d_recv, e_send, e_recv):
+                rs1, stage, rs2, cb, crecv, own, eb, cs, prod, erecv,
+                in_sem, t_send, t_recv, r_send, r_recv, c_send, c_recv, o_send, o_recv, d_send, d_recv, e_send, e_recv):
     rows, cols = nv.shape
     rank = bv.shape[1]
     tiles = cols // LANES
@@ -68,6 +68,7 @@
     core, far_chip = (leaf, p ^ 1), (leaf, p ^ 2)
     following, before = (leaf, lax.rem(p + 1, parts)), (leaf, lax.rem(p + parts - 1, parts))
     siblings = [(leaf ^ (1 << l), p) for l in range(levels)]
+    across_chip = (leaf ^ (1 << top), p ^ 2)
 
     def load(src, dst, i):
         copy = pltpu.make_async_copy(src, dst, in_sem.at[i])
@@ -81,7 +82,7 @@
         return copy
 
     barrier = pltpu.get_barrier_semaphore()
-    greeted = [core, far_chip, (leaf, p ^ 3)] + siblings
+    greeted = [core, far_chip, (leaf, p ^ 3), across_chip] + siblings
     for other in greeted:
         pl.semaphore_signal(barrier, inc=1, device_id=other, device_id_type=MESH)
     addr_v[...] = row_address(order_in[...], tiles)
@@ -227,12 +228,9 @@
         at = pl.multiple_of(i * CHUNK, CHUNK)
         split_out[pl.ds(2 * at, 2 * CHUNK), :] = stack(bv[pl.ds(at, CHUNK), :])
 
-    for l in range(top):
-        moved[l].wait_recv()
-        wt[top + l, 0], wt[top + l, 1] = split(tsib[l])
-
     edges = []
     up = []
+    over = []
     for h in range(PIECES):
         to_far[h].wait_recv()
         cb[0, hs[h], :] = cin[p, hs[h], :] + (rs1[1, hs[h], :] + rs2[hs[h], :])
@@ -244,38 +242,52 @@
         own[...] = three(dot, stack(cb[l]), wt[l, 0], wt[l, 1])
         weight(l)
         near_step(1 + l)
+        moved[l].wait_recv()
+        wt[top + l, 0], wt[top + l, 1] = split(tsib[l])
         for h in range(PIECES):
             up[l * PIECES + h].wait_recv()
             cb[l + 1, hs[h], :] = own[hs[h], :] + three(dot, stack(crecv[l, hs[h], :]), wt[top + l, 0], wt[top + l, 1])
-            up.append(send(cb.at[l + 1, hs[h]], crecv.at[l + 1, hs[h]], siblings[l + 1], c_send.at[l + 1, h], c_recv.at[l + 1, h]))
+            mine = cb.at[l + 1, hs[h]]
+            to = crecv.at[l + 1, hs[h]] if l + 1 < top else cs.at[p, hs[h]]
+            up.append(send(mine, to, siblings[l + 1], c_send.at[l + 1, h], c_recv.at[l + 1, h]))
+            if l + 1 == top:
+                over.append(send(mine, to, across_chip, o_send.at[h], o_recv.at[h]))
         part = three(dot_t, stack(crecv[l]), ws[l, 0], ws[l, 1])
-        ebuf[...] = part if l == 0 else ebuf[...] + part
+        eb[p] = part if l == 0 else eb[p] + part
+
+    to_chip = [send(eb.at[p, hs[h]], eb.at[p, hs[h]], far_chip, d_send.at[0, h], d_recv.at[0, h]) for h in range(PIECES)]
+    turns = [send(eb.at[p], eb.at[p], core, d_send.at[1, 0], d_recv.at[1, 0])]
     weight(top)
     near_step(levels)
-    d0, d1, d2 = [], [], []
-    for h in range(PIECES):
-        up[top * PIECES + h].wait_recv()
-        dbuf[p, hs[h], :] = ebuf[hs[h], :] + three(dot_t, stack(crecv[top, hs[h], :]), ws[top, 0], ws[top, 1])
-        mine = dbuf.at[p, hs[h]]
-        d0.append(send(mine, mine, far_chip, d_send.at[0, h], d_recv.at[0, h]))
-        d1.append(send(mine, mine, core, d_send.at[1, h], d_recv.at[1, h]))
+    near_step(levels + 1)
+
+    def lower(q):
+        prod[q] = three(dot_t, stack(cs[q]), ws[top, 0], ws[top, 1])
+
+    for k, copies in enumerate((up[top * PIECES:], over)):
+        for copy in copies:
+            copy.wait_recv()
+        turns.append(send(cs.at[p ^ (2 * k)], cs.at[p ^ (2 * k)], core, d_send.at[1, 1 + k], d_recv.at[1, 1 + k]))
+        lower(p ^ (2 * k))
 
     for copy in edges:
         copy.wait_recv()
     ph[:size, :], pl_[:size, :] = split(jnp.where(p == 0, 0.0, erecv[0]))
     ph[size + rows:, :], pl_[size + rows:, :] = split(jnp.where(p == parts - 1, 0.0, erecv[1]))
     near(0, 1)
-    near_step(levels + 1)
     near(units - 1, 1)
     for h in range(PIECES):
-        d0[h].wait_recv()
-        other = dbuf.at[p ^ 2, hs[h]]
-        d2.append(send(other, other, core, d_send.at[2, h], d_recv.at[2, h]))
-    for copy in d1 + d2:
+        to_chip[h].wait_recv()
+        other = eb.at[p ^ 2, hs[h]]
+        turns.append(send(other, other, core, d_send.at[2, h], d_recv.at[2, h]))
+    for k in range(2):
+        turns[1 + k].wait_recv()
+        lower(p ^ (1 + 2 * k))
+    for copy in turns[:1] + turns[3:]:
         copy.wait_recv()
     for q in range(parts):
-        d_out[q * width:(q + 1) * width, :] = dbuf[q]
-    for copy in sent + up + edges + d0 + d1 + d2:
+        d_out[q * width:(q + 1) * width, :] = eb[q] + prod[q]
+    for copy in sent + up + over + edges + to_chip + turns:
         copy.wait_send()
 
 
@@ -298,7 +310,7 @@
         ((2 * (levels - 1), 2, rank, rank), BF16), ((levels, 2, rank, rank), BF16), ((rank, rank), F32),
         (order.shape, I32), None, ((SUB, LANES), F32), ((SUB, LANES), I32), None,
         ((2,) + part, F32), (part, F32), (part, F32), ((levels,) + part, F32), ((levels,) + part, F32),
-        (part, F32), (part, F32), ((parts,) + part, F32), ((2, size, cols), F32),
+        (part, F32), ((parts,) + part, F32), ((parts,) + part, F32), ((parts,) + part, F32), ((2, size, cols), F32),
     ]
     scratch = [pltpu.VMEM(*s) if s else None for s in scratch]
     scratch[19] = pltpu.SMEM(order.shape, I32)
@@ -310,7 +322,7 @@
         out_specs=(vmem, vmem, vmem),
         scratch_shapes=scratch + [
             dma((7,)), dma((levels - 1,)), dma((levels - 1,)), dma((3, PIECES)), dma((3, PIECES)),
-            dma((levels, PIECES)), dma((levels, PIECES)), dma((3, PIECES)), dma((3, PIECES)), dma((2,)), dma((2,)),
+            dma((levels, PIECES)), dma((levels, PIECES)), dma((PIECES,)), dma((PIECES,)), dma((3, PIECES)), dma((3, PIECES)), dma((2,)), dma((2,)),
         ],
         compiler_params=pltpu.CompilerParams(vmem_limit_bytes=48 * MIB, collective_id=0, has_side_effects=True),
         name="tree_near",

time: 62.6 us -> 60.3 us (0.963)
  Pallas kernels: 62.4 us -> 60.1 us
    pallas_call x1, Pallas kernels: 52 us -> 49.7 us  [tree_call(): pl.pallas_call(functools.partial(tree_kernel, levels), out_shape=(pltpu.V...]
where the time goes in v3:
time: 60.3 us; the launch traced here: 60.2 us
  Pallas kernels  60.1 us (100%)
    pallas_call x1, Pallas kernels, tree_call(): pl.pallas_call(functools.partial(tree_kernel, levels), out_shape=(pltpu.V...  49.7 us
    pallas_call x1, Pallas kernels, scatter_call(): pl.pallas_call(scatter_kernel, out_shape=jax.ShapeDtypeStruct((rows * til...  10.4 us

profile of v3, /device:TPU:1, one launch (start us, length us, event | category | flops | bytes accessed | tf_op | source)
XLA Modules:
  0.0 60.2 jit_solution(702211137795809710)
XLA Ops:
  0.0 0.0 copy-start
  0.0 49.7 %tree_near.1 = (f32[512,256]{1,0:T(8,128)S(1)}, f32[4096,512]{1,0:T(8,128)S(1)}, bf16[8192,256]{1,0:T(8,128)(2,1)S(1)}) custom-call(s32[32,128]{1,0:T(8,128)} %bitcast.14, s32[2,64]{1,0:T(2,128)} %bitcast.19, f32[16384,128]{1,0:T(8,128)} %bitcast.16, f32[4096,256]{1,0:T(8,128)} %basis_hbm.1, f32[64,128,128]{2,1,0:T(8,128)} %blocks_hbm.1, ...), custom_call_target="tpu_custom_call" | custom-call | tf_op jit(solution)/shard_map/tree_near/pallas_call | solution.py:318
  49.7 0.0 copy-done
  49.8 10.4 %far_scatter.1 = f32[16384,128]{1,0:T(8,128)} custom-call(s32[32,128]{1,0:T(8,128)S(1)} %bitcast.15, f32[512,256]{1,0:T(8,128)S(1)} %get-tuple-element.8.d_in, bf16[8192,256]{1,0:T(8,128)(2,1)S(1)} %get-tuple-element.9.basis, f32[4096,512]{1,0:T(8,128)S(1)} %get-tuple-element.10.near), custom_call_target="tpu_custom_call" | custom-call | tf_op jit(solution)/shard_map/far_scatter/pallas_call | solution.py:379
Async XLA Ops:
  0.0 49.7 %copy-start = (s32[1,4096]{1,0:T(1,128)S(1)}, s32[1,4096]{1,0:T(1,128)}, u32[]{:S(2)}) copy-start(s32[1,4096]{1,0:T(1,128)} %param.8) | copy-start | bytes 49156

commit v4 on v3

--- a/solution.py
+++ b/solution.py
@@ -51,7 +51,7 @@
 
 
 def tree_kernel(levels, order_in, pairs_in, x_hbm, basis_hbm, blocks_hbm, t_hbm, g_hbm, d_out, nv, split_out,
-                xv, bv, bt, rows_a, rows_b, acc, cin, edge, ph, pl_, blk, pre,
+                xv, bv, rows_a, rows_b, acc, cin, edge, ph, pl_, blk, pre,
                 tv, gv, tsib, wt, ws, wf, addr_v, addr, key_v, tab_v, tab,
                 rs1, stage, rs2, cb, crecv, own, eb, cs, prod, erecv,
                 in_sem, t_send, t_recv, r_send, r_recv, c_send, c_recv, o_send, o_recv, d_send, d_recv, e_send, e_recv):
@@ -87,8 +87,8 @@
         pl.semaphore_signal(barrier, inc=1, device_id=other, device_id_type=MESH)
     addr_v[...] = row_address(order_in[...], tiles)
     in_a = load(addr_v, addr, 5)
+    in_x = load(x_hbm, xv, 3)
     in_b = load(basis_hbm, bv, 2)
-    in_x = load(x_hbm, xv, 3)
     in_t = load(t_hbm, tv, 0)
     in_g = load(g_hbm, gv, 1)
     in_k = load(blocks_hbm, blk, 4)
@@ -116,13 +116,6 @@
     pre[0] = jnp.zeros((size, size), F32)
     pre[count] = jnp.zeros((size, size), F32)
     acc[...] = jnp.zeros_like(acc)
-    in_b.wait()
-
-    @pl.loop(0, chunks)
-    def _(i):
-        at = pl.multiple_of(i * CHUNK, CHUNK)
-        bt[:, pl.ds(at, CHUNK)] = stack(bv[pl.ds(at, CHUNK), :].T)
-
     in_a.wait()
     in_tab.wait()
     in_x.wait()
@@ -142,9 +135,10 @@
         to = pl.ds(pl.multiple_of(size + at, size), CHUNK)
         ph[to, :] = hi
         pl_[to, :] = lo
-        acc[...] += three(dot, bt[:, pl.ds(at, CHUNK)], hi, lo)
+        acc[...] += three(dot, stack(bv[pl.ds(at, CHUNK), :].T), hi, lo)
 
     gather(0, rows_a)
+    in_b.wait()
     pl.semaphore_wait(barrier, len(greeted))
     moved = [send(t_hbm.at[l], tsib.at[l], siblings[l], t_send.at[l], t_recv.at[l]) for l in range(top)]
     for j, part in enumerate(tiles_of(rows_a, tiles, 0, size)):
@@ -164,10 +158,12 @@
     compress(chunks - 1, rows_b)
 
     hs = [pl.ds(h * piece, piece) for h in range(PIECES)]
-    for q in range(parts):
-        cin[q] = acc[:, q * width:(q + 1) * width].T
-    to_core = [[send(cin.at[p ^ (3 - 2 * k), hs[h]], rs1.at[k, hs[h]], core, r_send.at[k, h], r_recv.at[k, h])
-                for h in range(PIECES)] for k in range(2)]
+    to_core = []
+    for k, q in enumerate((p ^ 3, p ^ 1, p ^ 2, p)):
+        cin[q] = acc[:, pl.ds(pl.multiple_of(q * width, width), width)].T
+        if k < 2:
+            to_core.append([send(cin.at[q, hs[h]], rs1.at[k, hs[h]], core, r_send.at[k, h], r_recv.at[k, h])
+                            for h in range(PIECES)])
     to_far = []
     for h in range(PIECES):
         to_core[0][h].wait_recv()
@@ -303,7 +299,7 @@
     part = (width, rank)
     padded = (rows + 2 * size, cols)
     scratch = [
-        (x.shape, F32), (basis.shape, F32), ((2 * rank, rows), BF16), ((CHUNK * tiles, LANES), F32), ((CHUNK * tiles, LANES), F32),
+        (x.shape, F32), (basis.shape, F32), ((CHUNK * tiles, LANES), F32), ((CHUNK * tiles, LANES), F32),
         ((rank, cols), F32), ((parts,) + part, F32), ((2, size, cols), F32), (padded, BF16), (padded, BF16),
         (blocks.shape, F32), ((count + 1, size, size), F32),
         (transfer.shape, F32), (coupling.shape, F32), (transfer.shape, F32),
@@ -313,8 +309,8 @@
         (part, F32), ((parts,) + part, F32), ((parts,) + part, F32), ((parts,) + part, F32), ((2, size, cols), F32),
     ]
     scratch = [pltpu.VMEM(*s) if s else None for s in scratch]
-    scratch[19] = pltpu.SMEM(order.shape, I32)
-    scratch[22] = pltpu.SMEM((SUB, LANES), I32)
+    scratch[18] = pltpu.SMEM(order.shape, I32)
+    scratch[21] = pltpu.SMEM((SUB, LANES), I32)
     return pl.pallas_call(
         functools.partial(tree_kernel, levels),
         out_shape=(pltpu.VMEM((cols, rank), F32), pltpu.VMEM((rows, cols), F32), pltpu.VMEM((2 * rows, rank), BF16)),

time: 60.3 us -> 59.7 us (0.990)
    pallas_call x1, Pallas kernels: 49.7 us -> 49.1 us  [tree_call(): pl.pallas_call(functools.partial(tree_kernel, levels), out_shape=(pltpu.V...]
where the time goes in v4:
time: 59.7 us; the launch traced here: 59.5 us
  Pallas kernels  59.5 us (100%)
    pallas_call x1, Pallas kernels, tree_call(): pl.pallas_call(functools.partial(tree_kernel, levels), out_shape=(pltpu.V...  49.1 us
    pallas_call x1, Pallas kernels, scatter_call(): pl.pallas_call(scatter_kernel, out_shape=jax.ShapeDtypeStruct((rows * til...  10.4 us

profile of v4, /device:TPU:1, one launch (start us, length us, event | category | flops | bytes accessed | tf_op | source)
XLA Modules:
  0.0 59.5 jit_solution(6161188052855739965)
XLA Ops:
  0.0 0.0 copy-start
  0.0 49.1 %tree_near.1 = (f32[512,256]{1,0:T(8,128)S(1)}, f32[4096,512]{1,0:T(8,128)S(1)}, bf16[8192,256]{1,0:T(8,128)(2,1)S(1)}) custom-call(s32[32,128]{1,0:T(8,128)} %bitcast.14, s32[2,64]{1,0:T(2,128)} %bitcast.19, f32[16384,128]{1,0:T(8,128)} %bitcast.16, f32[4096,256]{1,0:T(8,128)} %basis_hbm.1, f32[64,128,128]{2,1,0:T(8,128)} %blocks_hbm.1, ...), custom_call_target="tpu_custom_call" | custom-call | tf_op jit(solution)/shard_map/tree_near/pallas_call | solution.py:314
  49.1 0.0 copy-done
  49.1 10.4 %far_scatter.1 = f32[16384,128]{1,0:T(8,128)} custom-call(s32[32,128]{1,0:T(8,128)S(1)} %bitcast.15, f32[512,256]{1,0:T(8,128)S(1)} %get-tuple-element.8.d_in, bf16[8192,256]{1,0:T(8,128)(2,1)S(1)} %get-tuple-element.9.basis, f32[4096,512]{1,0:T(8,128)S(1)} %get-tuple-element.10.near), custom_call_target="tpu_custom_call" | custom-call | tf_op jit(solution)/shard_map/far_scatter/pallas_call | solution.py:375
Async XLA Ops:
  0.0 49.1 %copy-start = (s32[1,4096]{1,0:T(1,128)S(1)}, s32[1,4096]{1,0:T(1,128)}, u32[]{:S(2)}) copy-start(s32[1,4096]{1,0:T(1,128)} %param.8) | copy-start | bytes 49156
